TPU v7x, 512 devices: a whole 4x8x8 slice. The times are simulated.
512 devices in a mesh: ens: 2 (over core), lat: 32 (over z, x), chan: 8 (over y).
Axes of the slice: x: 4, y: 8, z: 8, core: 2. Of those that a mesh axis runs over, the one named last changes fastest.
Arguments:
- field: bfloat16 [2, 384, 128, 256], P('ens', 'chan', 'lat'), may hold values from -6 to 6
- cotangent: bfloat16 [2, 384, 128, 256], P('ens', 'chan', 'lat'), may hold values from -6 to 6
- spec_weight: float32 [2, 64, 384], P(None, None, 'chan'), may hold values from -8 to 8
- disco_coef: float32 [128, 9], replicated, may hold values from -2 to 2
- disco_weight: float32 [9, 384], P(None, 'chan'), may hold values from -5 to 5
- disco_rows: int32 [128, 9], replicated, may hold values from 0 to 127, as said below
- disco_shift: int32 [128, 9], replicated, may hold values from -8 to 8
- w_hidden: bfloat16 [384, 768], replicated, may hold values from -0.3125 to 0.3125
- w_output: bfloat16 [768, 384], replicated, may hold values from -0.21875 to 0.21875
Outputs:
- grad_field: bfloat16 [2, 384, 128, 256], P('ens', 'chan', 'lat')
- grad_spec_weight: float32 [2, 64, 384], P(None, None, 'chan')
- grad_disco_weight: float32 [9, 384], P(None, 'chan')
- grad_w_hidden: float32 [384, 768], P('lat')
- grad_w_output: float32 [768, 384], P('lat')
Inputs may be any that keep to these rules, and one draw needn't show every extreme that they name: Entry k of row i of disco_rows names a latitude row within 2 rows of i.
All inputs are finite; a program needn't handle non-finite values.
Results may differ from a plain program's by a relative error of at most 0.013.
Values may be sent and summed in bfloat16 or wider, within the bound.
A program may use at most 64 MiB of HBM per device.

v0:
```python
import math
import jax
import jax.numpy as jnp
from jax import lax
from jax.sharding import PartitionSpec as P

HALO = 2
SHIFT = 8
norm_eps = 1e-06
inv_root_two = 0.7071067811865476
inv_root_tau = 0.3989422804014327
highest = lax.Precision.HIGHEST


def padded_2(block, sides, width):
    for axis, dim in sides:
        count = lax.axis_size(axis)
        forward = [(i, i + 1) for i in range(count - 1)]
        backward = [(target, source) for source, target in forward]
        low = lax.ppermute(
            lax.slice_in_dim(block, block.shape[dim] - width, None, axis=dim), axis, forward
        )
        high = lax.ppermute(lax.slice_in_dim(block, 0, width, axis=dim), axis, backward)
        block = jnp.concatenate([low, block, high], axis=dim)
    return block


def colatitudes(lat_count):
    return (jnp.arange(lat_count, dtype=jnp.int32).astype(jnp.float32) + 0.5) * (
        math.pi / lat_count
    )


def legendre_rows(first_order, order_count, lat_count, degree_count):
    colatitude = colatitudes(lat_count)
    cosine = jnp.cos(colatitude)
    sine_rows = jnp.sin(colatitude)
    orders = (first_order + jnp.arange(order_count, dtype=jnp.int32)).astype(jnp.float32)
    log_start = 0.5 * (
        jnp.log((2.0 * orders + 1.0) / (4.0 * math.pi))
        + lax.lgamma(orders + 0.5)
        - lax.lgamma(orders + 1.0)
        - 0.5 * math.log(math.pi)
    )
    diagonal = jnp.exp(log_start[:, None] + orders[:, None] * jnp.log(sine_rows)[None, :])

    def advance(carry, degree):
        previous, before = carry
        degree_value = degree.astype(jnp.float32)
        above = degree_value > orders
        upper_term = jnp.where(above, 4.0 * degree_value * degree_value - 1.0, 1.0)
        lower_term = jnp.where(above, degree_value * degree_value - orders * orders, 1.0)
        factor = jnp.sqrt(upper_term / lower_term)
        behind = jnp.where(
            above, (degree_value - 1.0) * (degree_value - 1.0) - orders * orders, 0.0
        )
        damping = jnp.sqrt(behind / (4.0 * (degree_value - 1.0) * (degree_value - 1.0) - 1.0))
        recurred = factor[:, None] * (cosine[None, :] * previous - damping[:, None] * before)
        current = jnp.where(
            above[:, None], recurred, jnp.where((degree_value == orders)[:, None], diagonal, 0.0)
        )
        return ((current, previous), current)

    zero_rows = jnp.zeros((order_count, lat_count), jnp.float32)
    finish, stacked = lax.scan(
        advance, (zero_rows, zero_rows), jnp.arange(degree_count, dtype=jnp.int32), unroll=True
    )
    return jnp.transpose(stacked, (1, 0, 2))


def quadrature(lat_count, lon_count):
    return 2.0 * math.pi / lon_count * (math.pi / lat_count) * jnp.sin(colatitudes(lat_count))


def lon_tables(lon_count, mode_count):
    columns = jnp.arange(lon_count, dtype=jnp.int32)
    mode_ids = jnp.arange(mode_count, dtype=jnp.int32)
    phase_ids = columns[:, None] * mode_ids[None, :] % lon_count
    angles = phase_ids.astype(jnp.float32) * (2.0 * math.pi / lon_count)
    cosine = jnp.cos(angles)
    sine_part = jnp.sin(angles)
    forward = jnp.concatenate([cosine, -sine_part], axis=1).astype(jnp.bfloat16)
    doubled = jnp.where(mode_ids == 0, 1.0, 2.0).astype(jnp.float32)[None, :]
    inverse = jnp.transpose(
        jnp.concatenate([doubled * cosine, -doubled * sine_part], axis=1)
    ).astype(jnp.bfloat16)
    return (forward, inverse)


def apply_filter(coeffs, spec_weight):
    real_weight = jnp.transpose(spec_weight[0])[:, None, :]
    imag_weight = jnp.transpose(spec_weight[1])[:, None, :]
    real_part = coeffs[:, 0]
    imag_part = coeffs[:, 1]
    return jnp.stack(
        [
            real_weight * real_part - imag_weight * imag_part,
            real_weight * imag_part + imag_weight * real_part,
        ],
        axis=1,
    )


def filter_adjoint(grads, coeffs, spec_weight):
    real_weight = jnp.transpose(spec_weight[0])[:, None, :]
    imag_weight = jnp.transpose(spec_weight[1])[:, None, :]
    grad_real = grads[:, 0]
    grad_imag = grads[:, 1]
    real_part = coeffs[:, 0]
    imag_part = coeffs[:, 1]
    weight_zero = jnp.transpose(jnp.sum(grad_real * real_part + grad_imag * imag_part, axis=1))
    weight_one = jnp.transpose(jnp.sum(grad_imag * real_part - grad_real * imag_part, axis=1))
    adjoint_coeffs = jnp.stack(
        [
            real_weight * grad_real + imag_weight * grad_imag,
            real_weight * grad_imag - imag_weight * grad_real,
        ],
        axis=1,
    )
    return (adjoint_coeffs, jnp.stack([weight_zero, weight_one], axis=0))


def mlp_backward(mixed_rows, adjoint_rows, w_hidden, w_output):
    mixed32 = mixed_rows.astype(jnp.float32)
    rscale = lax.rsqrt(jnp.mean(mixed32 * mixed32, axis=0, keepdims=True) + norm_eps)
    normed32 = mixed32 * rscale
    normed = normed32.astype(jnp.bfloat16)
    preact = lax.dot_general(
        w_hidden, normed, (((0,), (0,)), ((), ())), preferred_element_type=jnp.float32
    )
    activated = jax.nn.gelu(preact, approximate=False).astype(jnp.bfloat16)
    grad_output = lax.dot_general(
        activated, adjoint_rows, (((1,), (1,)), ((), ())), preferred_element_type=jnp.float32
    )
    grad_act = lax.dot_general(
        w_output, adjoint_rows, (((1,), (0,)), ((), ())), preferred_element_type=jnp.float32
    )
    cumulative = 0.5 * (1.0 + lax.erf(preact * inv_root_two))
    density = jnp.exp(-0.5 * preact * preact) * inv_root_tau
    grad_pre = (grad_act * (cumulative + preact * density)).astype(jnp.bfloat16)
    grad_hidden = lax.dot_general(
        normed, grad_pre, (((1,), (1,)), ((), ())), preferred_element_type=jnp.float32
    )
    grad_normed = lax.dot_general(
        w_hidden, grad_pre, (((1,), (0,)), ((), ())), preferred_element_type=jnp.float32
    )
    grad_mixed = (
        rscale * (grad_normed - normed32 * jnp.mean(grad_normed * normed32, axis=0, keepdims=True))
    ).astype(jnp.bfloat16)
    return (grad_mixed, grad_hidden, grad_output)


def to_modes(spectrum):
    return lax.all_to_all(spectrum, "lat", split_axis=3, concat_axis=1, tiled=True)


def to_bands(spectrum):
    return lax.all_to_all(spectrum, "lat", split_axis=1, concat_axis=3, tiled=True)


def wrap_lon(values, width):
    return jnp.concatenate([values[:, :, -width:], values, values[:, :, :width]], axis=2)


def disco_kernel(rows_tab, shift_tab, coef_tab, centre, disco_weight):
    row_step = rows_tab - centre[:, None] + HALO
    lon_step = shift_tab + SHIFT
    reach = jnp.arange(2 * HALO + 1, dtype=jnp.int32)
    span = jnp.arange(2 * SHIFT + 1, dtype=jnp.int32)
    onehot = (
        (row_step[:, :, None, None] == reach[None, None, :, None])
        & (lon_step[:, :, None, None] == span[None, None, None, :])
    ).astype(jnp.float32)
    kernel = jnp.einsum("rk,rkpq,kc->crpq", coef_tab, onehot, disco_weight, precision=highest)
    return (onehot, kernel)


def shards(
    field,
    cotangent,
    spec_weight,
    disco_coef,
    disco_weight,
    disco_rows,
    disco_shift,
    w_hidden,
    w_output,
):
    member = field[0]
    adjoint_member = cotangent[0]
    channels, lat_rows, lon_count = member.shape
    band_count = lax.axis_size("lat")
    lat_count = lat_rows * band_count
    mode_count = lat_count // 2
    modes_here = mode_count // band_count
    band_index = lax.axis_index("lat")
    first_row = band_index * lat_rows
    forward, inverse = lon_tables(lon_count, mode_count)
    legendre = legendre_rows(band_index * modes_here, modes_here, lat_count, mode_count)
    weighted = legendre * quadrature(lat_count, lon_count)[None, None, :]
    grad_scale = 1.0 / math.sqrt(lax.axis_size("ens") * lat_count * lon_count)
    reach_count = 2 * HALO + 1
    span_count = 2 * SHIFT + 1
    adjoint_rows = lax.all_to_all(adjoint_member, "chan", split_axis=2, concat_axis=0, tiled=True)
    spectrum = jnp.dot(
        member.reshape(channels * lat_rows, lon_count), forward, preferred_element_type=jnp.float32
    )
    spectrum = spectrum.astype(jnp.bfloat16).reshape(channels, lat_rows, 2, mode_count)
    mode_block = to_modes(spectrum)
    coeffs = jnp.einsum(
        "citm,mli->ctml", mode_block.astype(jnp.float32), weighted, precision=highest
    )
    synthesis = jnp.einsum(
        "ctml,mli->citm", apply_filter(coeffs, spec_weight), legendre, precision=highest
    ).astype(jnp.bfloat16)
    band_block = to_bands(synthesis)
    spectral = jnp.dot(
        band_block.reshape(channels * lat_rows, 2 * mode_count),
        inverse,
        preferred_element_type=jnp.float32,
    )
    spectral = spectral.reshape(channels, lat_rows, lon_count)
    global_rows = first_row + jnp.arange(lat_rows, dtype=jnp.int32)
    rows_here = lax.dynamic_slice_in_dim(disco_rows, first_row, lat_rows, 0)
    shift_here = lax.dynamic_slice_in_dim(disco_shift, first_row, lat_rows, 0)
    coef_here = lax.dynamic_slice_in_dim(disco_coef, first_row, lat_rows, 0)
    onehot_here, kernel_here = disco_kernel(
        rows_here, shift_here, coef_here, global_rows, disco_weight
    )
    padded = padded_2(member, (("lat", 1),), HALO)
    wide_field = wrap_lon(padded, SHIFT)
    disco_out = jnp.zeros((channels, lat_rows, lon_count), jnp.float32)
    for reach in range(reach_count):
        for span in range(span_count):
            window = wide_field[:, reach : reach + lat_rows, span : span + lon_count].astype(
                jnp.float32
            )
            disco_out = disco_out + kernel_here[:, :, reach, span][:, :, None] * window
    mixed_field = (spectral + disco_out).astype(jnp.bfloat16)
    mixed_rows = lax.all_to_all(mixed_field, "chan", split_axis=2, concat_axis=0, tiled=True)
    all_channels = mixed_rows.shape[0]
    row_width = mixed_rows.shape[2]
    grad_rows, grad_hidden, grad_output = mlp_backward(
        mixed_rows.reshape(all_channels, lat_rows * row_width),
        adjoint_rows.reshape(all_channels, lat_rows * row_width),
        w_hidden,
        w_output,
    )
    grad_field = lax.all_to_all(
        grad_rows.reshape(all_channels, lat_rows, row_width),
        "chan",
        split_axis=0,
        concat_axis=2,
        tiled=True,
    )
    grad_synth = lax.dot_general(
        grad_field.reshape(channels * lat_rows, lon_count),
        inverse,
        (((1,), (1,)), ((), ())),
        preferred_element_type=jnp.float32,
    )
    grad_synth = grad_synth.astype(jnp.bfloat16).reshape(channels, lat_rows, 2, mode_count)
    grad_modes = to_modes(grad_synth)
    grad_filtered = jnp.einsum(
        "citm,mli->ctml", grad_modes.astype(jnp.float32), legendre, precision=highest
    )
    grad_coeffs, filter_part = filter_adjoint(grad_filtered, coeffs, spec_weight)
    grad_spectrum = jnp.einsum("ctml,mli->citm", grad_coeffs, weighted, precision=highest).astype(
        jnp.bfloat16
    )
    grad_lines = to_bands(grad_spectrum)
    spectral_back = lax.dot_general(
        grad_lines.reshape(channels * lat_rows, 2 * mode_count),
        forward,
        (((1,), (1,)), ((), ())),
        preferred_element_type=jnp.float32,
    )
    spectral_back = spectral_back.reshape(channels, lat_rows, lon_count)
    grad_wide = grad_field.astype(jnp.float32)
    reach_sums = []
    for reach in range(reach_count):
        span_sums = []
        for span in range(span_count):
            window = wide_field[:, reach : reach + lat_rows, span : span + lon_count].astype(
                jnp.float32
            )
            span_sums.append(jnp.sum(window * grad_wide, axis=2))
        reach_sums.append(jnp.stack(span_sums, axis=2))
    inner_sum = jnp.stack(reach_sums, axis=2)
    disco_part = jnp.einsum(
        "ik,ikpq,cipq->kc", coef_here, onehot_here, inner_sum, precision=highest
    )
    rimmed = padded_2(grad_field, (("lat", 1),), HALO)
    wide_grads = wrap_lon(rimmed, SHIFT)
    ext_count = lat_rows + 2 * HALO
    ext_rows = first_row - HALO + jnp.arange(ext_count, dtype=jnp.int32)
    rows_ext = lax.dynamic_slice_in_dim(
        jnp.pad(disco_rows, ((HALO, HALO), (0, 0))), first_row, ext_count, 0
    )
    shift_ext = lax.dynamic_slice_in_dim(
        jnp.pad(disco_shift, ((HALO, HALO), (0, 0))), first_row, ext_count, 0
    )
    coef_ext = lax.dynamic_slice_in_dim(
        jnp.pad(disco_coef, ((HALO, HALO), (0, 0))), first_row, ext_count, 0
    )
    onehot_ext, kernel_ext = disco_kernel(rows_ext, shift_ext, coef_ext, ext_rows, disco_weight)
    spread = jnp.zeros((channels, lat_rows, lon_count), jnp.float32)
    for reach in range(reach_count):
        row_start = 2 * HALO - reach
        for span in range(span_count):
            col_start = 2 * SHIFT - span
            window = wide_grads[
                :, row_start : row_start + lat_rows, col_start : col_start + lon_count
            ].astype(jnp.float32)
            spread = (
                spread
                + kernel_ext[:, row_start : row_start + lat_rows, reach, span][:, :, None] * window
            )
    grad_input = (adjoint_member.astype(jnp.float32) + spectral_back + spread).astype(jnp.bfloat16)
    filter_total, disco_total = lax.psum((filter_part, disco_part), ("ens", "lat"))
    total_hidden, total_output = lax.psum((grad_hidden, grad_output), ("ens", "lat", "chan"))
    hidden_rows = total_hidden.shape[0] // band_count
    output_rows = total_output.shape[0] // band_count
    share_hidden = lax.dynamic_slice_in_dim(total_hidden, band_index * hidden_rows, hidden_rows, 0)
    share_output = lax.dynamic_slice_in_dim(total_output, band_index * output_rows, output_rows, 0)
    return (
        grad_input[None],
        filter_total,
        disco_total * grad_scale,
        share_hidden * grad_scale,
        share_output * grad_scale,
    )


def solution(mesh):
    in_specs = (
        P("ens", "chan", "lat", None),
        P("ens", "chan", "lat", None),
        P(None, None, "chan"),
        P(),
        P(None, "chan"),
        P(),
        P(),
        P(),
        P(),
    )
    out_specs = (
        P("ens", "chan", "lat", None),
        P(None, None, "chan"),
        P(None, "chan"),
        P("lat", None),
        P("lat", None),
    )
    return jax.shard_map(shards, mesh=mesh, in_specs=in_specs, out_specs=out_specs, check_vma=False)
```

profile of v0, /device:TPU:256, one launch (start us, length us, event | category | flops | bytes accessed | tf_op | source)
XLA Modules:
  0.0 485.7 jit_solution(5748793667730272015)
XLA Ops:
  7.5 0.9 reshape_squeeze.3
  8.9 0.8 reshape.55196
  9.7 9.9 %all-to-all-start = ((bf16[32,2,384]{2,1,0:T(2,128)(2,1)}), bf16[32,2,384]{2,1,0:T(2,128)(2,1)S(1)}, u32[]{:S(2)}, u32[]{:S(2)}) async-start(bf16[32,2,384]{2,1,0:T(2,128)(2,1)} %reshape.55196), calls=%async_computation | async-start | bytes 98304 | tf_op jit(solution)/shard_map/all_to_all | solution.py:154
  19.6 3.4 collective-permute-start
  23.0 5.8 %collective-permute-start.1 = (bf16[48,2,256]{2,0,1:T(8,128)(2,1)S(1)}, bf16[48,2,256]{2,0,1:T(8,128)(2,1)S(1)}, u32[]{:S(2)}, u32[]{:S(2)}) collective-permute-start(bf16[48,2,256]{2,0,1:T(8,128)(2,1)S(1)} %get-tuple-element.536), channel_id=1, source_target_pairs={{8,0},{16,8},{24,16},{32,24},{40,32},{48,40},{56,48},{64,56},{72,6... | collective-permute-start | bytes 147464 | tf_op jit(solution)/shard_map/ppermute | solution.py:23
  28.8 0.7 fusion.693
  33.5 0.7 fusion.694
  45.7 0.7 fusion.695
  50.4 0.7 fusion.692
  74.1 0.6 fusion.684
  74.7 0.7 fusion.685
  75.4 0.7 fusion.686
  77.1 0.9 convolution_bitcast_fusion
  78.7 0.7 fusion.681
  85.0 1.0 reshape.55202
  86.0 0.7 copy.394
  88.0 0.8 reshape.55198
  89.2 7.4 %all-to-all-start.1 = ((bf16[32,2,384]{2,1,0:T(2,128)(2,1)}), bf16[32,2,384]{2,1,0:T(2,128)(2,1)S(1)}, u32[]{:S(2)}, u32[]{:S(2)}) async-start(bf16[32,2,384]{2,1,0:T(2,128)(2,1)} %reshape.55198), calls=%async_computation.1 | async-start | bytes 98304 | tf_op jit(solution)/shard_map/all_to_all | solution.py:158
  96.8 4.9 %all-to-all-done.1 = bf16[32,2,384]{2,1,0:T(2,128)(2,1)S(1)} async-done(((bf16[32,2,384]{2,1,0:T(2,128)(2,1)}), bf16[32,2,384]{2,1,0:T(2,128)(2,1)S(1)}, u32[]{:S(2)}, u32[]{:S(2)}) %all-to-all-start.1) | async-done | bytes 49184 | tf_op jit(solution)/shard_map/all_to_all | solution.py:158
  101.7 7.1 %all-to-all-start.3 = ((bf16[8,2,3072]{2,1,0:T(2,128)(2,1)}), bf16[8,2,3072]{2,1,0:T(2,128)(2,1)S(1)}, u32[]{:S(2)}, u32[]{:S(2)}) async-start(bf16[8,2,3072]{2,1,0:T(2,128)(2,1)} %reshape.55202), calls=%async_computation.3 | async-start | bytes 196608 | tf_op jit(solution)/shard_map/all_to_all | solution.py:204
  109.5 6.0 %fusion.2 = bf16[48,4,256]{2,0,1:T(8,128)(2,1)S(1)} fusion(bf16[48,4,128]{0,2,1:T(8,128)(2,1)S(1)} %bitcast.623, bf16[48,4,256]{2,0,1:T(8,128)(2,1)S(1)} %bitcast.596, f32[48,4]{0,1:T(4,128)S(1)} %bitcast.820, f32[48,4]{0,1:T(4,128)S(1)} %bitcast.821, f32[48,4]{0,1:T(4,128)S(1)} %bitcast.822, f32[48,4]{0,1:T(4,128)S(1)} %bitcast.823, ...), kind=kOutput, calls=%fused_computation.173 | convolution fusion | flops 25493504 | bytes 8339200 | tf_op jit(solution)/shard_map/dot_general | solution.py:217
  115.7 1.0 reshape.55200
  116.7 0.8 all-to-all-done.3
  117.6 6.4 %all-to-all-start.2 = ((bf16[8,2,3072]{2,1,0:T(2,128)(2,1)}), bf16[8,2,3072]{2,1,0:T(2,128)(2,1)S(1)}, u32[]{:S(2)}, u32[]{:S(2)}) async-start(bf16[8,2,3072]{2,1,0:T(2,128)(2,1)} %reshape.55200), calls=%async_computation.2 | async-start | bytes 196608 | tf_op jit(solution)/shard_map/all_to_all | solution.py:240
  123.9 0.6 fusion.682
  125.2 7.5 %all-to-all-done.2 = bf16[8,2,3072]{2,1,0:T(2,128)(2,1)S(1)} async-done(((bf16[8,2,3072]{2,1,0:T(2,128)(2,1)}), bf16[8,2,3072]{2,1,0:T(2,128)(2,1)S(1)}, u32[]{:S(2)}, u32[]{:S(2)}) %all-to-all-start.2) | async-done | bytes 98336 | tf_op jit(solution)/shard_map/all_to_all | solution.py:240
  134.6 2.0 fusion.24
  137.8 1.0 reshape.55204
  138.8 3.4 all-to-all-start.4
  142.5 1.5 fusion.613
  144.0 6.9 %all-to-all-done.4 = bf16[8,2,3072]{2,1,0:T(2,128)(2,1)S(1)} async-done(((bf16[8,2,3072]{2,1,0:T(2,128)(2,1)}), bf16[8,2,3072]{2,1,0:T(2,128)(2,1)S(1)}, u32[]{:S(2)}, u32[]{:S(2)}) %all-to-all-start.4) | async-done | bytes 98336 | tf_op jit(solution)/shard_map/all_to_all | solution.py:249
  152.1 1.1 fusion.210
  153.2 1.2 fusion.219
  154.4 1.1 fusion.209
  155.5 1.2 fusion.218
  157.4 0.8 reshape.55206
  158.3 8.6 %all-to-all-start.5 = ((bf16[32,2,384]{2,1,0:T(2,128)(2,1)}), bf16[32,2,384]{2,1,0:T(2,128)(2,1)S(1)}, u32[]{:S(2)}, u32[]{:S(2)}) async-start(bf16[32,2,384]{2,1,0:T(2,128)(2,1)} %reshape.55206), calls=%async_computation.5 | async-start | bytes 98304 | tf_op jit(solution)/shard_map/all_to_all | solution.py:154
  166.9 3.4 collective-permute-start.2
  170.3 5.8 %collective-permute-start.3 = (bf16[48,2,256]{2,0,1:T(8,128)(2,1)S(1)}, bf16[48,2,256]{2,0,1:T(8,128)(2,1)S(1)}, u32[]{:S(2)}, u32[]{:S(2)}) collective-permute-start(bf16[48,2,256]{2,0,1:T(8,128)(2,1)S(1)} %get-tuple-element.534), channel_id=1, source_target_pairs={{8,0},{16,8},{24,16},{32,24},{40,32},{48,40},{56,48},{64,56},{72,6... | collective-permute-start | bytes 147464 | tf_op jit(solution)/shard_map/ppermute | solution.py:23
  176.1 0.8 fusion.217
  177.3 0.7 convolution_bitcast_fusion.6
  179.5 0.8 reshape.55208
  180.3 10.2 %all-to-all-start.6 = ((bf16[32,2,384]{2,1,0:T(2,128)(2,1)}), bf16[32,2,384]{2,1,0:T(2,128)(2,1)S(1)}, u32[]{:S(2)}, u32[]{:S(2)}) async-start(bf16[32,2,384]{2,1,0:T(2,128)(2,1)} %reshape.55208), calls=%async_computation.6 | async-start | bytes 98304 | tf_op jit(solution)/shard_map/all_to_all | solution.py:158
  190.5 276.9 %all-reduce.4 = (f32[2,64,48]{1,2,0:T(8,128)}, f32[9,48]{1,0:T(8,128)S(1)}) all-reduce(f32[2,64,48]{1,2,0:T(8,128)S(1)} %pad_maximum_fusion.8, f32[9,48]{1,0:T(8,128)S(1)} %convolution_bitcast_fusion.6), channel_id=1, replica_groups=mesh['ens'=2,'lat'=32,'chan'=8] {'ens','lat'}, use_global_device_ids=true, to_apply=%region_5.6 | all-reduce | flops 6576 | bytes 52608 | tf_op jit(solution)/shard_map/psum | solution.py:320
  468.7 6.5 %fusion.4 = bf16[1,48,4,256]{3,1,2,0:T(8,128)(2,1)S(1)} fusion(bf16[48,4,128]{0,2,1:T(8,128)(2,1)S(1)} %bitcast.622, bf16[48,4,256]{2,0,1:T(8,128)(2,1)S(1)} %all_to_all.100, bf16[48,8,256]{2,0,1:T(8,128)(2,1)S(1)} %get-tuple-element.539, bf16[48,8,8]{2,0,1:T(8,128)(2,1)S(1)} %get-tuple-element.520, bf16[48,8,8]{2,0,1:T(8,128)(2,1)S(1)} %get-tuple-element.519, ...), kind=kOutput, calls=%fused_computation.177 | convolution fusion | flops 37191680 | bytes 1076992 | tf_op jit(solution)/shard_map/dot_general | solution.py:272
  475.2 0.7 copy.395
  475.9 1.5 dynamic-slice_multiply_fusion
  477.5 1.4 dynamic-slice_multiply_fusion.1
  (425 shorter events, 18.6 us)
Async XLA Ops:
  7.2 127.0 %copy-start = (bf16[384,768]{1,0:T(8,128)(2,1)S(1)}, bf16[384,768]{1,0:T(8,128)(2,1)}, u32[]{:S(2)}) copy-start(bf16[384,768]{1,0:T(8,128)(2,1)} %param.16) | copy-start | bytes 1769476
  8.6 64.8 %copy-start.82 = (f32[9,48]{1,0:T(8,128)S(1)}, f32[9,48]{1,0:T(8,128)}, u32[]{:S(2)}) copy-start(f32[9,48]{1,0:T(8,128)} %param.13) | copy-start | bytes 5188
  9.7 77.4 %all-to-all-start = ((bf16[32,2,384]{2,1,0:T(2,128)(2,1)}), bf16[32,2,384]{2,1,0:T(2,128)(2,1)S(1)}, u32[]{:S(2)}, u32[]{:S(2)}) async-start(bf16[32,2,384]{2,1,0:T(2,128)(2,1)} %reshape.55196), calls=%async_computation | async-start | bytes 98304 | tf_op jit(solution)/shard_map/all_to_all | solution.py:154
  19.6 67.3 %collective-permute-start = (bf16[48,2,256]{2,0,1:T(8,128)(2,1)S(1)}, bf16[48,2,256]{2,0,1:T(8,128)(2,1)S(1)}, u32[]{:S(2)}, u32[]{:S(2)}) collective-permute-start(bf16[48,2,256]{2,0,1:T(8,128)(2,1)S(1)} %get-tuple-element.537), channel_id=1, source_target_pairs={{0,8},{8,16},{16,24},{24,32},{32,40},{40,48},{48,56},{56,64},{64,7... | collective-permute-start | bytes 147464 | tf_op jit(solution)/shard_map/ppermute | solution.py:20
  23.0 63.9 %collective-permute-start.1 = (bf16[48,2,256]{2,0,1:T(8,128)(2,1)S(1)}, bf16[48,2,256]{2,0,1:T(8,128)(2,1)S(1)}, u32[]{:S(2)}, u32[]{:S(2)}) collective-permute-start(bf16[48,2,256]{2,0,1:T(8,128)(2,1)S(1)} %get-tuple-element.536), channel_id=1, source_target_pairs={{8,0},{16,8},{24,16},{32,24},{40,32},{48,40},{56,48},{64,56},{72,6... | collective-permute-start | bytes 147464 | tf_op jit(solution)/shard_map/ppermute | solution.py:23
  89.2 12.5 %all-to-all-start.1 = ((bf16[32,2,384]{2,1,0:T(2,128)(2,1)}), bf16[32,2,384]{2,1,0:T(2,128)(2,1)S(1)}, u32[]{:S(2)}, u32[]{:S(2)}) async-start(bf16[32,2,384]{2,1,0:T(2,128)(2,1)} %reshape.55198), calls=%async_computation.1 | async-start | bytes 98304 | tf_op jit(solution)/shard_map/all_to_all | solution.py:158
  101.7 15.8 %all-to-all-start.3 = ((bf16[8,2,3072]{2,1,0:T(2,128)(2,1)}), bf16[8,2,3072]{2,1,0:T(2,128)(2,1)S(1)}, u32[]{:S(2)}, u32[]{:S(2)}) async-start(bf16[8,2,3072]{2,1,0:T(2,128)(2,1)} %reshape.55202), calls=%async_computation.3 | async-start | bytes 196608 | tf_op jit(solution)/shard_map/all_to_all | solution.py:204
  117.6 15.1 %all-to-all-start.2 = ((bf16[8,2,3072]{2,1,0:T(2,128)(2,1)}), bf16[8,2,3072]{2,1,0:T(2,128)(2,1)S(1)}, u32[]{:S(2)}, u32[]{:S(2)}) async-start(bf16[8,2,3072]{2,1,0:T(2,128)(2,1)} %reshape.55200), calls=%async_computation.2 | async-start | bytes 196608 | tf_op jit(solution)/shard_map/all_to_all | solution.py:240
  138.8 12.0 %all-to-all-start.4 = ((bf16[8,2,3072]{2,1,0:T(2,128)(2,1)}), bf16[8,2,3072]{2,1,0:T(2,128)(2,1)S(1)}, u32[]{:S(2)}, u32[]{:S(2)}) async-start(bf16[8,2,3072]{2,1,0:T(2,128)(2,1)} %reshape.55204), calls=%async_computation.4 | async-start | bytes 196608 | tf_op jit(solution)/shard_map/all_to_all | solution.py:249
  142.2 333.7 %all-reduce.7.cloned.1.call-start = ((), (), s32[]{:S(2)}) async-start(), calls=%async_computation.7 | async-start | bytes 4718592 | tf_op jit(solution)/shard_map/psum | solution.py:321
  158.3 19.9 %all-to-all-start.5 = ((bf16[32,2,384]{2,1,0:T(2,128)(2,1)}), bf16[32,2,384]{2,1,0:T(2,128)(2,1)S(1)}, u32[]{:S(2)}, u32[]{:S(2)}) async-start(bf16[32,2,384]{2,1,0:T(2,128)(2,1)} %reshape.55206), calls=%async_computation.5 | async-start | bytes 98304 | tf_op jit(solution)/shard_map/all_to_all | solution.py:154
  166.9 11.1 %collective-permute-start.2 = (bf16[48,2,256]{2,0,1:T(8,128)(2,1)S(1)}, bf16[48,2,256]{2,0,1:T(8,128)(2,1)S(1)}, u32[]{:S(2)}, u32[]{:S(2)}) collective-permute-start(bf16[48,2,256]{2,0,1:T(8,128)(2,1)S(1)} %get-tuple-element.535), channel_id=1, source_target_pairs={{0,8},{8,16},{16,24},{24,32},{32,40},{40,48},{48,56},{56,64},{64,7... | collective-permute-start | bytes 147464 | tf_op jit(solution)/shard_map/ppermute | solution.py:20
  170.3 7.8 %collective-permute-start.3 = (bf16[48,2,256]{2,0,1:T(8,128)(2,1)S(1)}, bf16[48,2,256]{2,0,1:T(8,128)(2,1)S(1)}, u32[]{:S(2)}, u32[]{:S(2)}) collective-permute-start(bf16[48,2,256]{2,0,1:T(8,128)(2,1)S(1)} %get-tuple-element.534), channel_id=1, source_target_pairs={{8,0},{16,8},{24,16},{32,24},{40,32},{48,40},{56,48},{64,56},{72,6... | collective-permute-start | bytes 147464 | tf_op jit(solution)/shard_map/ppermute | solution.py:23
  178.8 289.6 %copy-start.7 = (f32[48,4,1,1]{0,3,2,1:T(1,128)S(1)}, f32[48,4,1,1]{0,3,2,1:T(1,128)}, u32[]{:S(2)}) copy-start(f32[48,4,1,1]{0,3,2,1:T(1,128)} %get-tuple-element.400) | copy-start | bytes 2308
  178.8 289.6 %copy-start.8 = (f32[48,4,1,1]{0,3,2,1:T(1,128)S(1)}, f32[48,4,1,1]{0,3,2,1:T(1,128)}, u32[]{:S(2)}) copy-start(f32[48,4,1,1]{0,3,2,1:T(1,128)} %get-tuple-element.401) | copy-start | bytes 2308
  178.8 289.6 %copy-start.9 = (f32[48,4,1,1]{0,3,2,1:T(1,128)S(1)}, f32[48,4,1,1]{0,3,2,1:T(1,128)}, u32[]{:S(2)}) copy-start(f32[48,4,1,1]{0,3,2,1:T(1,128)} %get-tuple-element.402) | copy-start | bytes 2308
  178.8 289.6 %copy-start.10 = (f32[48,4,1,1]{0,3,2,1:T(1,128)S(1)}, f32[48,4,1,1]{0,3,2,1:T(1,128)}, u32[]{:S(2)}) copy-start(f32[48,4,1,1]{0,3,2,1:T(1,128)} %get-tuple-element.403) | copy-start | bytes 2308
  178.8 289.6 %copy-start.11 = (f32[48,4,1,1]{0,3,2,1:T(1,128)S(1)}, f32[48,4,1,1]{0,3,2,1:T(1,128)}, u32[]{:S(2)}) copy-start(f32[48,4,1,1]{0,3,2,1:T(1,128)} %get-tuple-element.404) | copy-start | bytes 2308
  178.8 289.6 %copy-start.12 = (f32[48,4,1,1]{0,3,2,1:T(1,128)S(1)}, f32[48,4,1,1]{0,3,2,1:T(1,128)}, u32[]{:S(2)}) copy-start(f32[48,4,1,1]{0,3,2,1:T(1,128)} %get-tuple-element.405) | copy-start | bytes 2308
  178.8 289.6 %copy-start.13 = (f32[48,4,1,1]{0,3,2,1:T(1,128)S(1)}, f32[48,4,1,1]{0,3,2,1:T(1,128)}, u32[]{:S(2)}) copy-start(f32[48,4,1,1]{0,3,2,1:T(1,128)} %get-tuple-element.406) | copy-start | bytes 2308
  178.8 289.6 %copy-start.14 = (f32[48,4,1,1]{0,3,2,1:T(1,128)S(1)}, f32[48,4,1,1]{0,3,2,1:T(1,128)}, u32[]{:S(2)}) copy-start(f32[48,4,1,1]{0,3,2,1:T(1,128)} %get-tuple-element.407) | copy-start | bytes 2308
  178.9 289.6 %copy-start.15 = (f32[48,4,1,1]{0,3,2,1:T(1,128)S(1)}, f32[48,4,1,1]{0,3,2,1:T(1,128)}, u32[]{:S(2)}) copy-start(f32[48,4,1,1]{0,3,2,1:T(1,128)} %get-tuple-element.408) | copy-start | bytes 2308
  178.9 289.6 %copy-start.16 = (f32[48,4,1,1]{0,3,2,1:T(1,128)S(1)}, f32[48,4,1,1]{0,3,2,1:T(1,128)}, u32[]{:S(2)}) copy-start(f32[48,4,1,1]{0,3,2,1:T(1,128)} %get-tuple-element.409) | copy-start | bytes 2308
  178.9 289.6 %copy-start.17 = (f32[48,4,1,1]{0,3,2,1:T(1,128)S(1)}, f32[48,4,1,1]{0,3,2,1:T(1,128)}, u32[]{:S(2)}) copy-start(f32[48,4,1,1]{0,3,2,1:T(1,128)} %get-tuple-element.410) | copy-start | bytes 2308
  178.9 289.6 %copy-start.18 = (f32[48,4,1,1]{0,3,2,1:T(1,128)S(1)}, f32[48,4,1,1]{0,3,2,1:T(1,128)}, u32[]{:S(2)}) copy-start(f32[48,4,1,1]{0,3,2,1:T(1,128)} %get-tuple-element.411) | copy-start | bytes 2308
  178.9 289.6 %copy-start.19 = (f32[48,4,1,1]{0,3,2,1:T(1,128)S(1)}, f32[48,4,1,1]{0,3,2,1:T(1,128)}, u32[]{:S(2)}) copy-start(f32[48,4,1,1]{0,3,2,1:T(1,128)} %get-tuple-element.412) | copy-start | bytes 2308
  178.9 289.6 %copy-start.20 = (f32[48,4,1,1]{0,3,2,1:T(1,128)S(1)}, f32[48,4,1,1]{0,3,2,1:T(1,128)}, u32[]{:S(2)}) copy-start(f32[48,4,1,1]{0,3,2,1:T(1,128)} %get-tuple-element.413) | copy-start | bytes 2308
  178.9 289.6 %copy-start.21 = (f32[48,4,1,1]{0,3,2,1:T(1,128)S(1)}, f32[48,4,1,1]{0,3,2,1:T(1,128)}, u32[]{:S(2)}) copy-start(f32[48,4,1,1]{0,3,2,1:T(1,128)} %get-tuple-element.414) | copy-start | bytes 2308
  178.9 289.6 %copy-start.22 = (f32[48,4,1,1]{0,3,2,1:T(1,128)S(1)}, f32[48,4,1,1]{0,3,2,1:T(1,128)}, u32[]{:S(2)}) copy-start(f32[48,4,1,1]{0,3,2,1:T(1,128)} %get-tuple-element.415) | copy-start | bytes 2308
  178.9 289.6 %copy-start.23 = (f32[48,4,1,1]{0,3,2,1:T(1,128)S(1)}, f32[48,4,1,1]{0,3,2,1:T(1,128)}, u32[]{:S(2)}) copy-start(f32[48,4,1,1]{0,3,2,1:T(1,128)} %get-tuple-element.416) | copy-start | bytes 2308
  178.9 289.6 %copy-start.24 = (f32[48,4,1,1]{0,3,2,1:T(1,128)S(1)}, f32[48,4,1,1]{0,3,2,1:T(1,128)}, u32[]{:S(2)}) copy-start(f32[48,4,1,1]{0,3,2,1:T(1,128)} %get-tuple-element.417) | copy-start | bytes 2308
  179.0 289.6 %copy-start.25 = (f32[48,4,1,1]{0,3,2,1:T(1,128)S(1)}, f32[48,4,1,1]{0,3,2,1:T(1,128)}, u32[]{:S(2)}) copy-start(f32[48,4,1,1]{0,3,2,1:T(1,128)} %get-tuple-element.418) | copy-start | bytes 2308
  179.0 289.6 %copy-start.26 = (f32[48,4,1,1]{0,3,2,1:T(1,128)S(1)}, f32[48,4,1,1]{0,3,2,1:T(1,128)}, u32[]{:S(2)}) copy-start(f32[48,4,1,1]{0,3,2,1:T(1,128)} %get-tuple-element.419) | copy-start | bytes 2308
  179.0 289.6 %copy-start.27 = (f32[48,4,1,1]{0,3,2,1:T(1,128)S(1)}, f32[48,4,1,1]{0,3,2,1:T(1,128)}, u32[]{:S(2)}) copy-start(f32[48,4,1,1]{0,3,2,1:T(1,128)} %get-tuple-element.420) | copy-start | bytes 2308
  179.0 289.6 %copy-start.28 = (f32[48,4,1,1]{0,3,2,1:T(1,128)S(1)}, f32[48,4,1,1]{0,3,2,1:T(1,128)}, u32[]{:S(2)}) copy-start(f32[48,4,1,1]{0,3,2,1:T(1,128)} %get-tuple-element.421) | copy-start | bytes 2308
  179.0 289.6 %copy-start.29 = (f32[48,4,1,1]{0,3,2,1:T(1,128)S(1)}, f32[48,4,1,1]{0,3,2,1:T(1,128)}, u32[]{:S(2)}) copy-start(f32[48,4,1,1]{0,3,2,1:T(1,128)} %get-tuple-element.422) | copy-start | bytes 2308
  179.0 289.6 %copy-start.30 = (f32[48,4,1,1]{0,3,2,1:T(1,128)S(1)}, f32[48,4,1,1]{0,3,2,1:T(1,128)}, u32[]{:S(2)}) copy-start(f32[48,4,1,1]{0,3,2,1:T(1,128)} %get-tuple-element.423) | copy-start | bytes 2308
  179.0 289.6 %copy-start.31 = (f32[48,4,1,1]{0,3,2,1:T(1,128)S(1)}, f32[48,4,1,1]{0,3,2,1:T(1,128)}, u32[]{:S(2)}) copy-start(f32[48,4,1,1]{0,3,2,1:T(1,128)} %get-tuple-element.424) | copy-start | bytes 2308
  179.0 289.6 %copy-start.72 = (f32[48,4,1,1]{0,3,2,1:T(1,128)S(1)}, f32[48,4,1,1]{0,3,2,1:T(1,128)}, u32[]{:S(2)}) copy-start(f32[48,4,1,1]{0,3,2,1:T(1,128)} %get-tuple-element.425) | copy-start | bytes 2308
  179.0 289.6 %copy-start.73 = (f32[48,4,1,1]{0,3,2,1:T(1,128)S(1)}, f32[48,4,1,1]{0,3,2,1:T(1,128)}, u32[]{:S(2)}) copy-start(f32[48,4,1,1]{0,3,2,1:T(1,128)} %get-tuple-element.426) | copy-start | bytes 2308
  179.0 289.6 %copy-start.74 = (f32[48,4,1,1]{0,3,2,1:T(1,128)S(1)}, f32[48,4,1,1]{0,3,2,1:T(1,128)}, u32[]{:S(2)}) copy-start(f32[48,4,1,1]{0,3,2,1:T(1,128)} %get-tuple-element.427) | copy-start | bytes 2308
  179.1 289.6 %copy-start.75 = (f32[48,4,1,1]{0,3,2,1:T(1,128)S(1)}, f32[48,4,1,1]{0,3,2,1:T(1,128)}, u32[]{:S(2)}) copy-start(f32[48,4,1,1]{0,3,2,1:T(1,128)} %get-tuple-element.428) | copy-start | bytes 2308
  179.1 289.6 %copy-start.76 = (f32[48,4,1,1]{0,3,2,1:T(1,128)S(1)}, f32[48,4,1,1]{0,3,2,1:T(1,128)}, u32[]{:S(2)}) copy-start(f32[48,4,1,1]{0,3,2,1:T(1,128)} %get-tuple-element.429) | copy-start | bytes 2308
  179.1 289.6 %copy-start.77 = (f32[48,4,1,1]{0,3,2,1:T(1,128)S(1)}, f32[48,4,1,1]{0,3,2,1:T(1,128)}, u32[]{:S(2)}) copy-start(f32[48,4,1,1]{0,3,2,1:T(1,128)} %get-tuple-element.430) | copy-start | bytes 2308
  179.1 289.6 %copy-start.78 = (f32[48,4,1,1]{0,3,2,1:T(1,128)S(1)}, f32[48,4,1,1]{0,3,2,1:T(1,128)}, u32[]{:S(2)}) copy-start(f32[48,4,1,1]{0,3,2,1:T(1,128)} %get-tuple-element.431) | copy-start | bytes 2308
  179.1 289.6 %copy-start.79 = (f32[48,4,1,1]{0,3,2,1:T(1,128)S(1)}, f32[48,4,1,1]{0,3,2,1:T(1,128)}, u32[]{:S(2)}) copy-start(f32[48,4,1,1]{0,3,2,1:T(1,128)} %get-tuple-element.432) | copy-start | bytes 2308
  179.1 289.6 %copy-start.80 = (f32[48,4,1,1]{0,3,2,1:T(1,128)S(1)}, f32[48,4,1,1]{0,3,2,1:T(1,128)}, u32[]{:S(2)}) copy-start(f32[48,4,1,1]{0,3,2,1:T(1,128)} %get-tuple-element.433) | copy-start | bytes 2308
  180.3 287.7 %all-to-all-start.6 = ((bf16[32,2,384]{2,1,0:T(2,128)(2,1)}), bf16[32,2,384]{2,1,0:T(2,128)(2,1)S(1)}, u32[]{:S(2)}, u32[]{:S(2)}) async-start(bf16[32,2,384]{2,1,0:T(2,128)(2,1)} %reshape.55208), calls=%async_computation.6 | async-start | bytes 98304 | tf_op jit(solution)/shard_map/all_to_all | solution.py:158
  (47 other events, 1021.5 us)
Sparse Core Ops, SparseCore 0:
  148.1 279.6 all-reduce.6
where the time goes:
time: 487 us; the launch traced here: 486 us
  blocking collectives  277 us (57%)
  starting transfers between devices  71.5 us (15%)
  between operations  58.2 us (12%)
  local copies, waits for them, and re-layouts  24.1 us (5%)
  matrix products  20.6 us (4%)
  waiting for transfers between devices  20.2 us (4%)
  other arithmetic  14.3 us (3%)
    psum x1, blocking collectives, shards(): lax.psum((filter_part, disco_part), ('ens', 'lat'))  277 us
    all_to_all x2, starting transfers between devices, to_modes(): lax.all_to_all(spectrum, 'lat', split_axis=3, concat_axis=1, tiled=True)  18.5 us
    all_to_all x2, starting transfers between devices, to_bands(): lax.all_to_all(spectrum, 'lat', split_axis=1, concat_axis=3, tiled=True)  17.6 us
    ppermute x2, starting transfers between devices, padded_2(): lax.ppermute(lax.slice_in_dim(block, 0, width, axis=dim), axis, backward)  11.6 us
  transfers between devices with their start and end apart: 12, of which 4 were waited for; matrix products, arithmetic and copies ran while one was open for 9% of the time, Pallas kernels for 0%

commit v1 on v0

--- a/solution.py
+++ b/solution.py
@@ -10,6 +10,23 @@
 inv_root_two = 0.7071067811865476
 inv_root_tau = 0.3989422804014327
 highest = lax.Precision.HIGHEST
+
+
+def track_stages_all(obj, k_dim, tile_in):
+    z2 = obj.shape
+    w1 = jnp.moveaxis(
+        obj.reshape(*z2[:k_dim], tile_in, z2[k_dim] // tile_in, *z2[k_dim + 1 :]), k_dim, 0
+    )
+    return w1
+
+
+def settle_the_scenes(here_x, row_dim):
+    here_x = jnp.moveaxis(here_x, 0, row_dim)
+    carry_out = here_x.shape
+    val2 = here_x.reshape(
+        *carry_out[:row_dim], carry_out[row_dim] * carry_out[row_dim + 1], *carry_out[row_dim + 2 :]
+    )
+    return val2
 
 
 def padded_2(block, sides, width):
@@ -237,7 +254,18 @@
             )
             disco_out = disco_out + kernel_here[:, :, reach, span][:, :, None] * window
     mixed_field = (spectral + disco_out).astype(jnp.bfloat16)
-    mixed_rows = lax.all_to_all(mixed_field, "chan", split_axis=2, concat_axis=0, tiled=True)
+    mat_out, item_now = (lax.psum(1, "chan"), lax.axis_index("chan"))
+    part_now = track_stages_all(mixed_field, 2, mat_out)
+    it = 1
+    gallery = [part_now[item_now]]
+    while it < mat_out:
+        then = part_now[item_now ^ it]
+        gallery.append(
+            lax.ppermute(then, axis_name="chan", perm=[(s, s ^ it) for s in range(mat_out)])
+        )
+        it = it + 1
+    part_now = jnp.stack(gallery, 0)[item_now ^ jnp.arange(mat_out)]
+    mixed_rows = settle_the_scenes(part_now, 0)
     all_channels = mixed_rows.shape[0]
     row_width = mixed_rows.shape[2]
     grad_rows, grad_hidden, grad_output = mlp_backward(

time: 487 us -> 512 us (1.051)
  starting transfers between devices: 71.5 us -> 93.8 us
    ppermute x0 -> x7, starting transfers between devices: none -> 26.9 us  [shards(): lax.ppermute(then, axis_name='chan', perm=[(s, s ^ it) for s in range(mat...]
    all_to_all x1 -> x0, waiting for transfers between devices: 7.47 us -> none  [shards(): lax.all_to_all(mixed_field, 'chan', split_axis=2, concat_axis=0, tiled=True)]
    all_to_all x1 -> x0, starting transfers between devices: 6.38 us -> none  [shards(): lax.all_to_all(mixed_field, 'chan', split_axis=2, concat_axis=0, tiled=True)]
    all_to_all x1, waiting for transfers between devices: 0.83 us -> 6.93 us  [shards(): lax.all_to_all(adjoint_member, 'chan', split_axis=2, concat_axis=0, tiled...]
  transfers between devices with their start and end apart: 12 -> 18, of which waited for: 4 -> 4; matrix products, arithmetic and copies ran while one was open for 9% -> 8% of each run, Pallas kernels for 0% -> 0%
where the time goes in v1:
time: 512 us; the launch traced here: 511 us
  blocking collectives  277 us (54%)
  starting transfers between devices  93.8 us (18%)
  between operations  57.8 us (11%)
  local copies, waits for them, and re-layouts  25.7 us (5%)
  matrix products  21.8 us (4%)
  waiting for transfers between devices  20 us (4%)
  other arithmetic  14.4 us (3%)
    psum x1, blocking collectives, shards(): lax.psum((filter_part, disco_part), ('ens', 'lat'))  277 us
    ppermute x7, starting transfers between devices, shards(): lax.ppermute(then, axis_name='chan', perm=[(s, s ^ it) for s in range(mat...  26.9 us
    all_to_all x2, starting transfers between devices, to_modes(): lax.all_to_all(spectrum, 'lat', split_axis=3, concat_axis=1, tiled=True)  18.5 us
    all_to_all x2, starting transfers between devices, to_bands(): lax.all_to_all(spectrum, 'lat', split_axis=1, concat_axis=3, tiled=True)  17.6 us
    ppermute x2, starting transfers between devices, padded_2(): lax.ppermute(lax.slice_in_dim(block, 0, width, axis=dim), axis, backward)  11.6 us
  transfers between devices with their start and end apart: 18, of which 4 were waited for; matrix products, arithmetic and copies ran while one was open for 8% of the time, Pallas kernels for 0%

profile of v1, /device:TPU:256, one launch (start us, length us, event | category | flops | bytes accessed | tf_op | source)
XLA Modules:
  0.0 510.5 jit_solution(10365059083648567608)
XLA Ops:
  7.5 0.9 reshape_squeeze.3
  8.9 0.8 reshape.55231
  9.7 9.9 %all-to-all-start = ((bf16[32,2,384]{2,1,0:T(2,128)(2,1)}), bf16[32,2,384]{2,1,0:T(2,128)(2,1)S(1)}, u32[]{:S(2)}, u32[]{:S(2)}) async-start(bf16[32,2,384]{2,1,0:T(2,128)(2,1)} %reshape.55231), calls=%async_computation | async-start | bytes 98304 | tf_op jit(solution)/shard_map/all_to_all | solution.py:171
  19.6 3.4 collective-permute-start
  23.0 5.8 %collective-permute-start.1 = (bf16[48,2,256]{2,0,1:T(8,128)(2,1)S(1)}, bf16[48,2,256]{2,0,1:T(8,128)(2,1)S(1)}, u32[]{:S(2)}, u32[]{:S(2)}) collective-permute-start(bf16[48,2,256]{2,0,1:T(8,128)(2,1)S(1)} %get-tuple-element.534), channel_id=1, source_target_pairs={{8,0},{16,8},{24,16},{32,24},{40,32},{48,40},{56,48},{64,56},{72,6... | collective-permute-start | bytes 147464 | tf_op jit(solution)/shard_map/ppermute | solution.py:40
  28.8 0.7 fusion.697
  33.4 0.7 fusion.698
  49.8 0.7 fusion.696
  74.1 0.7 fusion.688
  77.1 0.9 convolution_bitcast_fusion
  79.3 0.7 fusion.685
  86.3 1.0 reshape.55235
  88.4 7.1 %all-to-all-start.2 = ((bf16[8,2,3072]{2,1,0:T(2,128)(2,1)}), bf16[8,2,3072]{2,1,0:T(2,128)(2,1)S(1)}, u32[]{:S(2)}, u32[]{:S(2)}) async-start(bf16[8,2,3072]{2,1,0:T(2,128)(2,1)} %reshape.55235), calls=%async_computation.2 | async-start | bytes 196608 | tf_op jit(solution)/shard_map/all_to_all | solution.py:221
  96.5 0.8 reshape.55233
  97.3 6.9 %all-to-all-done.2 = bf16[8,2,3072]{2,1,0:T(2,128)(2,1)S(1)} async-done(((bf16[8,2,3072]{2,1,0:T(2,128)(2,1)}), bf16[8,2,3072]{2,1,0:T(2,128)(2,1)S(1)}, u32[]{:S(2)}, u32[]{:S(2)}) %all-to-all-start.2) | async-done | bytes 98336 | tf_op jit(solution)/shard_map/all_to_all | solution.py:221
  104.3 7.4 %all-to-all-start.1 = ((bf16[32,2,384]{2,1,0:T(2,128)(2,1)}), bf16[32,2,384]{2,1,0:T(2,128)(2,1)S(1)}, u32[]{:S(2)}, u32[]{:S(2)}) async-start(bf16[32,2,384]{2,1,0:T(2,128)(2,1)} %reshape.55233), calls=%async_computation.1 | async-start | bytes 98304 | tf_op jit(solution)/shard_map/all_to_all | solution.py:175
  112.8 3.9 all-to-all-done.1
  117.5 6.3 %fusion.2 = bf16[48,4,256]{2,0,1:T(8,128)(2,1)S(1)} fusion(bf16[48,4,128]{0,2,1:T(8,128)(2,1)S(1)} %bitcast.640, bf16[48,4,256]{2,0,1:T(8,128)(2,1)S(1)} %bitcast.616, f32[48,4]{0,1:T(4,128)S(1)} %bitcast.853, f32[48,4]{0,1:T(4,128)S(1)} %bitcast.854, f32[48,4]{0,1:T(4,128)S(1)} %bitcast.855, f32[48,4]{0,1:T(4,128)S(1)} %bitcast.856, ...), kind=kOutput, calls=%fused_computation.174 | convolution fusion | flops 25493504 | bytes 8339200 | tf_op jit(solution)/shard_map/dot_general | solution.py:234
  124.0 0.8 constant_dynamic-slice_fusion
  125.0 2.5 collective-permute-start.2
  127.6 2.2 collective-permute-start.3
  129.9 5.4 %collective-permute-start.4 = (bf16[48,4,32]{0,2,1:T(8,128)(2,1)S(1)}, bf16[48,4,32]{0,2,1:T(8,128)(2,1)S(1)}, u32[]{:S(2)}, u32[]{:S(2)}) collective-permute-start(bf16[48,4,32]{0,2,1:T(8,128)(2,1)S(1)} %bitcast.647), channel_id=1, source_target_pairs={{0,3},{1,2},{2,1},{3,0},{4,7},{5,6},{6,5},{7,4},{8,11},{9,10},{10,... | collective-permute-start | bytes 36872 | tf_op jit(solution)/shard_map/ppermute | solution.py:264
  135.5 2.5 collective-permute-start.5
  138.1 5.5 %collective-permute-start.6 = (bf16[48,4,32]{0,2,1:T(8,128)(2,1)S(1)}, bf16[48,4,32]{0,2,1:T(8,128)(2,1)S(1)}, u32[]{:S(2)}, u32[]{:S(2)}) collective-permute-start(bf16[48,4,32]{0,2,1:T(8,128)(2,1)S(1)} %bitcast.645), channel_id=1, source_target_pairs={{0,5},{1,4},{2,7},{3,6},{4,1},{5,0},{6,3},{7,2},{8,13},{9,12},{10,... | collective-permute-start | bytes 36872 | tf_op jit(solution)/shard_map/ppermute | solution.py:264
  143.8 4.1 collective-permute-start.7
  147.9 4.8 collective-permute-start.8
  152.8 2.1 collective-permute-done.8
  156.6 2.0 fusion.24
  159.7 1.0 reshape.55237
  160.8 5.1 %all-to-all-start.3 = ((bf16[8,2,3072]{2,1,0:T(2,128)(2,1)}), bf16[8,2,3072]{2,1,0:T(2,128)(2,1)S(1)}, u32[]{:S(2)}, u32[]{:S(2)}) async-start(bf16[8,2,3072]{2,1,0:T(2,128)(2,1)} %reshape.55237), calls=%async_computation.3 | async-start | bytes 196608 | tf_op jit(solution)/shard_map/all_to_all | solution.py:277
  166.2 1.5 fusion.617
  167.7 7.0 %all-to-all-done.3 = bf16[8,2,3072]{2,1,0:T(2,128)(2,1)S(1)} async-done(((bf16[8,2,3072]{2,1,0:T(2,128)(2,1)}), bf16[8,2,3072]{2,1,0:T(2,128)(2,1)S(1)}, u32[]{:S(2)}, u32[]{:S(2)}) %all-to-all-start.3) | async-done | bytes 98336 | tf_op jit(solution)/shard_map/all_to_all | solution.py:277
  175.9 1.1 fusion.210
  177.0 1.2 fusion.219
  178.2 1.1 fusion.209
  179.3 1.2 fusion.218
  181.2 0.8 reshape.55239
  182.1 8.6 %all-to-all-start.4 = ((bf16[32,2,384]{2,1,0:T(2,128)(2,1)}), bf16[32,2,384]{2,1,0:T(2,128)(2,1)S(1)}, u32[]{:S(2)}, u32[]{:S(2)}) async-start(bf16[32,2,384]{2,1,0:T(2,128)(2,1)} %reshape.55239), calls=%async_computation.4 | async-start | bytes 98304 | tf_op jit(solution)/shard_map/all_to_all | solution.py:171
  190.7 3.4 collective-permute-start.9
  194.1 5.8 %collective-permute-start.10 = (bf16[48,2,256]{2,0,1:T(8,128)(2,1)S(1)}, bf16[48,2,256]{2,0,1:T(8,128)(2,1)S(1)}, u32[]{:S(2)}, u32[]{:S(2)}) collective-permute-start(bf16[48,2,256]{2,0,1:T(8,128)(2,1)S(1)} %get-tuple-element.532), channel_id=1, source_target_pairs={{8,0},{16,8},{24,16},{32,24},{40,32},{48,40},{56,48},{64,56},{72,6... | collective-permute-start | bytes 147464 | tf_op jit(solution)/shard_map/ppermute | solution.py:40
  199.9 0.8 fusion.217
  203.4 0.8 reshape.55241
  204.2 10.2 %all-to-all-start.5 = ((bf16[32,2,384]{2,1,0:T(2,128)(2,1)}), bf16[32,2,384]{2,1,0:T(2,128)(2,1)S(1)}, u32[]{:S(2)}, u32[]{:S(2)}) async-start(bf16[32,2,384]{2,1,0:T(2,128)(2,1)} %reshape.55241), calls=%async_computation.5 | async-start | bytes 98304 | tf_op jit(solution)/shard_map/all_to_all | solution.py:175
  214.4 276.9 %all-reduce.4 = (f32[2,64,48]{1,2,0:T(8,128)}, f32[9,48]{1,0:T(8,128)S(1)}) all-reduce(f32[2,64,48]{1,2,0:T(8,128)S(1)} %pad_maximum_fusion.8, f32[9,48]{1,0:T(8,128)S(1)} %convolution_bitcast_fusion.6), channel_id=1, replica_groups=mesh['ens'=2,'lat'=32,'chan'=8] {'ens','lat'}, use_global_device_ids=true, to_apply=%region_4.5 | all-reduce | flops 6576 | bytes 52608 | tf_op jit(solution)/shard_map/psum | solution.py:348
  492.6 7.4 %fusion.4 = bf16[1,48,4,256]{3,1,2,0:T(8,128)(2,1)S(1)} fusion(bf16[48,4,128]{0,2,1:T(8,128)(2,1)S(1)} %bitcast.639, bf16[48,4,256]{2,0,1:T(8,128)(2,1)S(1)} %all_to_all.92, bf16[48,8,256]{2,0,1:T(8,128)(2,1)S(1)} %get-tuple-element.537, bf16[48,8,8]{2,0,1:T(8,128)(2,1)S(1)} %get-tuple-element.518, bf16[48,8,8]{2,0,1:T(8,128)(2,1)S(1)} %get-tuple-element.517, ...), kind=kOutput, calls=%fused_computation.178 | convolution fusion | flops 37191680 | bytes 1076992 | tf_op jit(solution)/shard_map/dot_general | solution.py:300
  500.1 0.7 copy.275
  500.8 1.5 dynamic-slice_multiply_fusion
  502.3 1.4 dynamic-slice_multiply_fusion.1
  (462 shorter events, 24.5 us)
Async XLA Ops:
  9.7 78.7 %all-to-all-start = ((bf16[32,2,384]{2,1,0:T(2,128)(2,1)}), bf16[32,2,384]{2,1,0:T(2,128)(2,1)S(1)}, u32[]{:S(2)}, u32[]{:S(2)}) async-start(bf16[32,2,384]{2,1,0:T(2,128)(2,1)} %reshape.55231), calls=%async_computation | async-start | bytes 98304 | tf_op jit(solution)/shard_map/all_to_all | solution.py:171
  19.6 68.6 %collective-permute-start = (bf16[48,2,256]{2,0,1:T(8,128)(2,1)S(1)}, bf16[48,2,256]{2,0,1:T(8,128)(2,1)S(1)}, u32[]{:S(2)}, u32[]{:S(2)}) collective-permute-start(bf16[48,2,256]{2,0,1:T(8,128)(2,1)S(1)} %get-tuple-element.535), channel_id=1, source_target_pairs={{0,8},{8,16},{16,24},{24,32},{32,40},{40,48},{48,56},{56,64},{64,7... | collective-permute-start | bytes 147464 | tf_op jit(solution)/shard_map/ppermute | solution.py:37
  23.0 65.3 %collective-permute-start.1 = (bf16[48,2,256]{2,0,1:T(8,128)(2,1)S(1)}, bf16[48,2,256]{2,0,1:T(8,128)(2,1)S(1)}, u32[]{:S(2)}, u32[]{:S(2)}) collective-permute-start(bf16[48,2,256]{2,0,1:T(8,128)(2,1)S(1)} %get-tuple-element.534), channel_id=1, source_target_pairs={{8,0},{16,8},{24,16},{32,24},{40,32},{48,40},{56,48},{64,56},{72,6... | collective-permute-start | bytes 147464 | tf_op jit(solution)/shard_map/ppermute | solution.py:40
  88.4 15.9 %all-to-all-start.2 = ((bf16[8,2,3072]{2,1,0:T(2,128)(2,1)}), bf16[8,2,3072]{2,1,0:T(2,128)(2,1)S(1)}, u32[]{:S(2)}, u32[]{:S(2)}) async-start(bf16[8,2,3072]{2,1,0:T(2,128)(2,1)} %reshape.55235), calls=%async_computation.2 | async-start | bytes 196608 | tf_op jit(solution)/shard_map/all_to_all | solution.py:221
  104.3 12.5 %all-to-all-start.1 = ((bf16[32,2,384]{2,1,0:T(2,128)(2,1)}), bf16[32,2,384]{2,1,0:T(2,128)(2,1)S(1)}, u32[]{:S(2)}, u32[]{:S(2)}) async-start(bf16[32,2,384]{2,1,0:T(2,128)(2,1)} %reshape.55233), calls=%async_computation.1 | async-start | bytes 98304 | tf_op jit(solution)/shard_map/all_to_all | solution.py:175
  125.0 18.7 %collective-permute-start.2 = (bf16[48,4,32]{0,2,1:T(8,128)(2,1)S(1)}, bf16[48,4,32]{0,2,1:T(8,128)(2,1)S(1)}, u32[]{:S(2)}, u32[]{:S(2)}) collective-permute-start(bf16[48,4,32]{0,2,1:T(8,128)(2,1)S(1)} %bitcast.649), channel_id=1, source_target_pairs={{0,1},{1,0},{2,3},{3,2},{4,5},{5,4},{6,7},{7,6},{8,9},{9,8},{10,11... | collective-permute-start | bytes 36872 | tf_op jit(solution)/shard_map/ppermute | solution.py:264
  127.6 20.3 %collective-permute-start.3 = (bf16[48,4,32]{0,2,1:T(8,128)(2,1)S(1)}, bf16[48,4,32]{0,2,1:T(8,128)(2,1)S(1)}, u32[]{:S(2)}, u32[]{:S(2)}) collective-permute-start(bf16[48,4,32]{0,2,1:T(8,128)(2,1)S(1)} %bitcast.648), channel_id=1, source_target_pairs={{0,2},{1,3},{2,0},{3,1},{4,6},{5,7},{6,4},{7,5},{8,10},{9,11},{10,... | collective-permute-start | bytes 36872 | tf_op jit(solution)/shard_map/ppermute | solution.py:264
  129.9 22.7 %collective-permute-start.4 = (bf16[48,4,32]{0,2,1:T(8,128)(2,1)S(1)}, bf16[48,4,32]{0,2,1:T(8,128)(2,1)S(1)}, u32[]{:S(2)}, u32[]{:S(2)}) collective-permute-start(bf16[48,4,32]{0,2,1:T(8,128)(2,1)S(1)} %bitcast.647), channel_id=1, source_target_pairs={{0,3},{1,2},{2,1},{3,0},{4,7},{5,6},{6,5},{7,4},{8,11},{9,10},{10,... | collective-permute-start | bytes 36872 | tf_op jit(solution)/shard_map/ppermute | solution.py:264
  135.5 17.2 %collective-permute-start.5 = (bf16[48,4,32]{0,2,1:T(8,128)(2,1)S(1)}, bf16[48,4,32]{0,2,1:T(8,128)(2,1)S(1)}, u32[]{:S(2)}, u32[]{:S(2)}) collective-permute-start(bf16[48,4,32]{0,2,1:T(8,128)(2,1)S(1)} %bitcast.646), channel_id=1, source_target_pairs={{0,4},{1,5},{2,6},{3,7},{4,0},{5,1},{6,2},{7,3},{8,12},{9,13},{10,... | collective-permute-start | bytes 36872 | tf_op jit(solution)/shard_map/ppermute | solution.py:264
  138.1 14.7 %collective-permute-start.6 = (bf16[48,4,32]{0,2,1:T(8,128)(2,1)S(1)}, bf16[48,4,32]{0,2,1:T(8,128)(2,1)S(1)}, u32[]{:S(2)}, u32[]{:S(2)}) collective-permute-start(bf16[48,4,32]{0,2,1:T(8,128)(2,1)S(1)} %bitcast.645), channel_id=1, source_target_pairs={{0,5},{1,4},{2,7},{3,6},{4,1},{5,0},{6,3},{7,2},{8,13},{9,12},{10,... | collective-permute-start | bytes 36872 | tf_op jit(solution)/shard_map/ppermute | solution.py:264
  143.8 9.0 %collective-permute-start.7 = (bf16[48,4,32]{0,2,1:T(8,128)(2,1)S(1)}, bf16[48,4,32]{0,2,1:T(8,128)(2,1)S(1)}, u32[]{:S(2)}, u32[]{:S(2)}) collective-permute-start(bf16[48,4,32]{0,2,1:T(8,128)(2,1)S(1)} %bitcast.644), channel_id=1, source_target_pairs={{0,6},{1,7},{2,4},{3,5},{4,2},{5,3},{6,0},{7,1},{8,14},{9,15},{10,... | collective-permute-start | bytes 36872 | tf_op jit(solution)/shard_map/ppermute | solution.py:264
  147.9 7.0 %collective-permute-start.8 = (bf16[48,4,32]{0,2,1:T(8,128)(2,1)S(1)}, bf16[48,4,32]{0,2,1:T(8,128)(2,1)S(1)}, u32[]{:S(2)}, u32[]{:S(2)}) collective-permute-start(bf16[48,4,32]{0,2,1:T(8,128)(2,1)S(1)} %bitcast.643), channel_id=1, source_target_pairs={{0,7},{1,6},{2,5},{3,4},{4,3},{5,2},{6,1},{7,0},{8,15},{9,14},{10,... | collective-permute-start | bytes 36872 | tf_op jit(solution)/shard_map/ppermute | solution.py:264
  160.8 13.9 %all-to-all-start.3 = ((bf16[8,2,3072]{2,1,0:T(2,128)(2,1)}), bf16[8,2,3072]{2,1,0:T(2,128)(2,1)S(1)}, u32[]{:S(2)}, u32[]{:S(2)}) async-start(bf16[8,2,3072]{2,1,0:T(2,128)(2,1)} %reshape.55237), calls=%async_computation.3 | async-start | bytes 196608 | tf_op jit(solution)/shard_map/all_to_all | solution.py:277
  165.9 334.9 %all-reduce.7.cloned.1.call-start = ((), (), s32[]{:S(2)}) async-start(), calls=%async_computation.6 | async-start | bytes 4718592 | tf_op jit(solution)/shard_map/psum | solution.py:349
  182.1 19.9 %all-to-all-start.4 = ((bf16[32,2,384]{2,1,0:T(2,128)(2,1)}), bf16[32,2,384]{2,1,0:T(2,128)(2,1)S(1)}, u32[]{:S(2)}, u32[]{:S(2)}) async-start(bf16[32,2,384]{2,1,0:T(2,128)(2,1)} %reshape.55239), calls=%async_computation.4 | async-start | bytes 98304 | tf_op jit(solution)/shard_map/all_to_all | solution.py:171
  190.7 11.1 %collective-permute-start.9 = (bf16[48,2,256]{2,0,1:T(8,128)(2,1)S(1)}, bf16[48,2,256]{2,0,1:T(8,128)(2,1)S(1)}, u32[]{:S(2)}, u32[]{:S(2)}) collective-permute-start(bf16[48,2,256]{2,0,1:T(8,128)(2,1)S(1)} %get-tuple-element.533), channel_id=1, source_target_pairs={{0,8},{8,16},{16,24},{24,32},{32,40},{40,48},{48,56},{56,64},{64,7... | collective-permute-start | bytes 147464 | tf_op jit(solution)/shard_map/ppermute | solution.py:37
  194.1 7.8 %collective-permute-start.10 = (bf16[48,2,256]{2,0,1:T(8,128)(2,1)S(1)}, bf16[48,2,256]{2,0,1:T(8,128)(2,1)S(1)}, u32[]{:S(2)}, u32[]{:S(2)}) collective-permute-start(bf16[48,2,256]{2,0,1:T(8,128)(2,1)S(1)} %get-tuple-element.532), channel_id=1, source_target_pairs={{8,0},{16,8},{24,16},{32,24},{40,32},{48,40},{56,48},{64,56},{72,6... | collective-permute-start | bytes 147464 | tf_op jit(solution)/shard_map/ppermute | solution.py:40
  202.6 289.7 %copy-start.7 = (f32[48,4,1,1]{0,3,2,1:T(1,128)S(1)}, f32[48,4,1,1]{0,3,2,1:T(1,128)}, u32[]{:S(2)}) copy-start(f32[48,4,1,1]{0,3,2,1:T(1,128)} %get-tuple-element.371) | copy-start | bytes 2308
  202.6 289.7 %copy-start.8 = (f32[48,4,1,1]{0,3,2,1:T(1,128)S(1)}, f32[48,4,1,1]{0,3,2,1:T(1,128)}, u32[]{:S(2)}) copy-start(f32[48,4,1,1]{0,3,2,1:T(1,128)} %get-tuple-element.372) | copy-start | bytes 2308
  202.6 289.7 %copy-start.9 = (f32[48,4,1,1]{0,3,2,1:T(1,128)S(1)}, f32[48,4,1,1]{0,3,2,1:T(1,128)}, u32[]{:S(2)}) copy-start(f32[48,4,1,1]{0,3,2,1:T(1,128)} %get-tuple-element.373) | copy-start | bytes 2308
  202.6 289.7 %copy-start.10 = (f32[48,4,1,1]{0,3,2,1:T(1,128)S(1)}, f32[48,4,1,1]{0,3,2,1:T(1,128)}, u32[]{:S(2)}) copy-start(f32[48,4,1,1]{0,3,2,1:T(1,128)} %get-tuple-element.374) | copy-start | bytes 2308
  202.6 289.7 %copy-start.11 = (f32[48,4,1,1]{0,3,2,1:T(1,128)S(1)}, f32[48,4,1,1]{0,3,2,1:T(1,128)}, u32[]{:S(2)}) copy-start(f32[48,4,1,1]{0,3,2,1:T(1,128)} %get-tuple-element.375) | copy-start | bytes 2308
  202.6 289.7 %copy-start.12 = (f32[48,4,1,1]{0,3,2,1:T(1,128)S(1)}, f32[48,4,1,1]{0,3,2,1:T(1,128)}, u32[]{:S(2)}) copy-start(f32[48,4,1,1]{0,3,2,1:T(1,128)} %get-tuple-element.376) | copy-start | bytes 2308
  202.6 289.7 %copy-start.13 = (f32[48,4,1,1]{0,3,2,1:T(1,128)S(1)}, f32[48,4,1,1]{0,3,2,1:T(1,128)}, u32[]{:S(2)}) copy-start(f32[48,4,1,1]{0,3,2,1:T(1,128)} %get-tuple-element.377) | copy-start | bytes 2308
  202.6 289.7 %copy-start.14 = (f32[48,4,1,1]{0,3,2,1:T(1,128)S(1)}, f32[48,4,1,1]{0,3,2,1:T(1,128)}, u32[]{:S(2)}) copy-start(f32[48,4,1,1]{0,3,2,1:T(1,128)} %get-tuple-element.378) | copy-start | bytes 2308
  202.6 289.7 %copy-start.15 = (f32[48,4,1,1]{0,3,2,1:T(1,128)S(1)}, f32[48,4,1,1]{0,3,2,1:T(1,128)}, u32[]{:S(2)}) copy-start(f32[48,4,1,1]{0,3,2,1:T(1,128)} %get-tuple-element.379) | copy-start | bytes 2308
  202.7 289.7 %copy-start.16 = (f32[48,4,1,1]{0,3,2,1:T(1,128)S(1)}, f32[48,4,1,1]{0,3,2,1:T(1,128)}, u32[]{:S(2)}) copy-start(f32[48,4,1,1]{0,3,2,1:T(1,128)} %get-tuple-element.380) | copy-start | bytes 2308
  202.7 289.7 %copy-start.17 = (f32[48,4,1,1]{0,3,2,1:T(1,128)S(1)}, f32[48,4,1,1]{0,3,2,1:T(1,128)}, u32[]{:S(2)}) copy-start(f32[48,4,1,1]{0,3,2,1:T(1,128)} %get-tuple-element.381) | copy-start | bytes 2308
  202.7 289.7 %copy-start.18 = (f32[48,4,1,1]{0,3,2,1:T(1,128)S(1)}, f32[48,4,1,1]{0,3,2,1:T(1,128)}, u32[]{:S(2)}) copy-start(f32[48,4,1,1]{0,3,2,1:T(1,128)} %get-tuple-element.382) | copy-start | bytes 2308
  202.7 289.7 %copy-start.19 = (f32[48,4,1,1]{0,3,2,1:T(1,128)S(1)}, f32[48,4,1,1]{0,3,2,1:T(1,128)}, u32[]{:S(2)}) copy-start(f32[48,4,1,1]{0,3,2,1:T(1,128)} %get-tuple-element.383) | copy-start | bytes 2308
  202.7 289.7 %copy-start.20 = (f32[48,4,1,1]{0,3,2,1:T(1,128)S(1)}, f32[48,4,1,1]{0,3,2,1:T(1,128)}, u32[]{:S(2)}) copy-start(f32[48,4,1,1]{0,3,2,1:T(1,128)} %get-tuple-element.384) | copy-start | bytes 2308
  202.7 289.7 %copy-start.21 = (f32[48,4,1,1]{0,3,2,1:T(1,128)S(1)}, f32[48,4,1,1]{0,3,2,1:T(1,128)}, u32[]{:S(2)}) copy-start(f32[48,4,1,1]{0,3,2,1:T(1,128)} %get-tuple-element.385) | copy-start | bytes 2308
  202.7 289.7 %copy-start.22 = (f32[48,4,1,1]{0,3,2,1:T(1,128)S(1)}, f32[48,4,1,1]{0,3,2,1:T(1,128)}, u32[]{:S(2)}) copy-start(f32[48,4,1,1]{0,3,2,1:T(1,128)} %get-tuple-element.386) | copy-start | bytes 2308
  202.7 289.7 %copy-start.23 = (f32[48,4,1,1]{0,3,2,1:T(1,128)S(1)}, f32[48,4,1,1]{0,3,2,1:T(1,128)}, u32[]{:S(2)}) copy-start(f32[48,4,1,1]{0,3,2,1:T(1,128)} %get-tuple-element.387) | copy-start | bytes 2308
  202.7 289.7 %copy-start.24 = (f32[48,4,1,1]{0,3,2,1:T(1,128)S(1)}, f32[48,4,1,1]{0,3,2,1:T(1,128)}, u32[]{:S(2)}) copy-start(f32[48,4,1,1]{0,3,2,1:T(1,128)} %get-tuple-element.388) | copy-start | bytes 2308
  202.7 289.7 %copy-start.25 = (f32[48,4,1,1]{0,3,2,1:T(1,128)S(1)}, f32[48,4,1,1]{0,3,2,1:T(1,128)}, u32[]{:S(2)}) copy-start(f32[48,4,1,1]{0,3,2,1:T(1,128)} %get-tuple-element.389) | copy-start | bytes 2308
  202.8 289.7 %copy-start.26 = (f32[48,4,1,1]{0,3,2,1:T(1,128)S(1)}, f32[48,4,1,1]{0,3,2,1:T(1,128)}, u32[]{:S(2)}) copy-start(f32[48,4,1,1]{0,3,2,1:T(1,128)} %get-tuple-element.390) | copy-start | bytes 2308
  202.8 289.7 %copy-start.27 = (f32[48,4,1,1]{0,3,2,1:T(1,128)S(1)}, f32[48,4,1,1]{0,3,2,1:T(1,128)}, u32[]{:S(2)}) copy-start(f32[48,4,1,1]{0,3,2,1:T(1,128)} %get-tuple-element.391) | copy-start | bytes 2308
  202.8 289.7 %copy-start.28 = (f32[48,4,1,1]{0,3,2,1:T(1,128)S(1)}, f32[48,4,1,1]{0,3,2,1:T(1,128)}, u32[]{:S(2)}) copy-start(f32[48,4,1,1]{0,3,2,1:T(1,128)} %get-tuple-element.392) | copy-start | bytes 2308
  202.8 289.7 %copy-start.29 = (f32[48,4,1,1]{0,3,2,1:T(1,128)S(1)}, f32[48,4,1,1]{0,3,2,1:T(1,128)}, u32[]{:S(2)}) copy-start(f32[48,4,1,1]{0,3,2,1:T(1,128)} %get-tuple-element.393) | copy-start | bytes 2308
  202.8 289.7 %copy-start.30 = (f32[48,4,1,1]{0,3,2,1:T(1,128)S(1)}, f32[48,4,1,1]{0,3,2,1:T(1,128)}, u32[]{:S(2)}) copy-start(f32[48,4,1,1]{0,3,2,1:T(1,128)} %get-tuple-element.394) | copy-start | bytes 2308
  202.8 289.7 %copy-start.31 = (f32[48,4,1,1]{0,3,2,1:T(1,128)S(1)}, f32[48,4,1,1]{0,3,2,1:T(1,128)}, u32[]{:S(2)}) copy-start(f32[48,4,1,1]{0,3,2,1:T(1,128)} %get-tuple-element.395) | copy-start | bytes 2308
  202.8 289.7 %copy-start.32 = (f32[48,4,1,1]{0,3,2,1:T(1,128)S(1)}, f32[48,4,1,1]{0,3,2,1:T(1,128)}, u32[]{:S(2)}) copy-start(f32[48,4,1,1]{0,3,2,1:T(1,128)} %get-tuple-element.396) | copy-start | bytes 2308
  202.8 289.7 %copy-start.33 = (f32[48,4,1,1]{0,3,2,1:T(1,128)S(1)}, f32[48,4,1,1]{0,3,2,1:T(1,128)}, u32[]{:S(2)}) copy-start(f32[48,4,1,1]{0,3,2,1:T(1,128)} %get-tuple-element.397) | copy-start | bytes 2308
  202.8 289.7 %copy-start.34 = (f32[48,4,1,1]{0,3,2,1:T(1,128)S(1)}, f32[48,4,1,1]{0,3,2,1:T(1,128)}, u32[]{:S(2)}) copy-start(f32[48,4,1,1]{0,3,2,1:T(1,128)} %get-tuple-element.398) | copy-start | bytes 2308
  202.8 289.7 %copy-start.35 = (f32[48,4,1,1]{0,3,2,1:T(1,128)S(1)}, f32[48,4,1,1]{0,3,2,1:T(1,128)}, u32[]{:S(2)}) copy-start(f32[48,4,1,1]{0,3,2,1:T(1,128)} %get-tuple-element.399) | copy-start | bytes 2308
  202.9 289.7 %copy-start.36 = (f32[48,4,1,1]{0,3,2,1:T(1,128)S(1)}, f32[48,4,1,1]{0,3,2,1:T(1,128)}, u32[]{:S(2)}) copy-start(f32[48,4,1,1]{0,3,2,1:T(1,128)} %get-tuple-element.400) | copy-start | bytes 2308
  204.2 287.7 %all-to-all-start.5 = ((bf16[32,2,384]{2,1,0:T(2,128)(2,1)}), bf16[32,2,384]{2,1,0:T(2,128)(2,1)S(1)}, u32[]{:S(2)}, u32[]{:S(2)}) async-start(bf16[32,2,384]{2,1,0:T(2,128)(2,1)} %reshape.55241), calls=%async_computation.5 | async-start | bytes 98304 | tf_op jit(solution)/shard_map/all_to_all | solution.py:175
  (59 other events, 3545.6 us)
Sparse Core Ops, SparseCore 0:
  171.8 280.0 all-reduce.6
